TPU v7x, 256 devices: a whole 4x4x8 slice. The times are simulated.
256 devices in a mesh: seq: 4 (over y), vocab: 64 (over z, x, core).
Axes of the slice: x: 4, y: 4, z: 8, core: 2. Of those that a mesh axis runs over, the one named last changes fastest.
Arguments:
- hidden: bfloat16 [2048, 2048], P('seq', 'vocab')
- tangent: bfloat16 [2048, 2048], P('seq', 'vocab'), may hold values from -6 to 6
- head_weight: bfloat16 [2048, 76032], P(None, 'vocab'), as said below
- weight_dir: bfloat16 [2048, 76032], P(None, 'vocab'), may hold values from -0.125 to 0.125
Outputs:
- grad_hidden: float32 [2048, 2048], P('seq', 'vocab')
- grad_weight: float32 [2048, 76032], P('seq', 'vocab')
Inputs may be any that keep to these rules, and one draw needn't show every extreme that they name: `head_weight`: columns of the head have scales of order one that differ between entries.
All inputs are finite; a program needn't handle non-finite values.
Results may differ from a plain program's by a relative error of at most 0.0029.
Values may be sent and summed in bfloat16 or wider, within the bound.
No kernel may reach another device: no remote copies, remote signals or barrier semaphores. Data moves between devices by JAX's collectives and lax.ppermute only.
A program may use at most 128 MiB of HBM per device.

v0:
```python
import jax
import jax.numpy as jnp
from jax import lax
from jax.sharding import PartitionSpec as P


def per_device(hidden, tangent, head_weight, weight_dir):
    full_hidden, full_tangent = (
        lax.all_gather(hidden, "vocab", axis=1, tiled=True),
        lax.all_gather(tangent, "vocab", axis=1, tiled=True),
    )
    logits = jnp.dot(full_hidden, head_weight, preferred_element_type=jnp.float32)
    moved = jnp.dot(full_tangent, head_weight, preferred_element_type=jnp.float32) + jnp.dot(
        full_hidden, weight_dir, preferred_element_type=jnp.float32
    )
    top = lax.pmax(jnp.max(logits, axis=1, keepdims=True), "vocab")
    scaled = jnp.exp(logits - top)
    total, weighted = lax.psum(
        (jnp.sum(scaled, axis=1, keepdims=True), jnp.sum(scaled * moved, axis=1, keepdims=True)),
        "vocab",
    )
    probe = (scaled / total * (moved - weighted / total)).astype(jnp.bfloat16)
    grad_cols = lax.psum_scatter(
        lax.dot_general(
            head_weight, probe, (((1,), (1,)), ((), ())), preferred_element_type=jnp.float32
        ),
        "vocab",
        scatter_dimension=0,
        tiled=True,
    )
    grad_hidden = grad_cols.T
    grad_weight = lax.psum_scatter(
        lax.dot_general(
            full_hidden, probe, (((0,), (0,)), ((), ())), preferred_element_type=jnp.float32
        ),
        "seq",
        scatter_dimension=0,
        tiled=True,
    )
    return (grad_hidden, grad_weight)


def solution(mesh):
    placed = (P("seq", "vocab"), P("seq", "vocab"), P(None, "vocab"), P(None, "vocab"))
    return jax.shard_map(
        per_device,
        mesh=mesh,
        in_specs=placed,
        out_specs=(P("seq", "vocab"), P("seq", "vocab")),
        check_vma=False,
    )
```

profile of v0, /device:TPU:1, one launch (start us, length us, event | category | flops | bytes accessed | tf_op | source)
XLA Modules:
  0.0 619.4 jit_solution(12880957579192441965)
XLA Ops:
  7.2 0.0 all-gather.3.cloned.1.call-start
  7.2 0.7 all-gather.3.cloned.1.call-update
  7.9 0.0 all-gather.5.cloned.1.call-start
  7.9 0.7 all-gather.5.cloned.1.call-update
  8.6 0.0 reduce-scatter.7.cloned.1.call-start
  8.7 83.5 %all-gather.3.cloned.1.call-done = bf16[512,2048]{0,1:T(8,128)(2,1)} async-done(((bf16[512,32]{0,1:T(8,128)(2,1)}), bf16[512,2048]{0,1:T(8,128)(2,1)}) %all-gather.3.cloned.1.call-update) | async-done | bytes 2097168 | tf_op jit(solution)/shard_map/all_gather | solution.py:9
  92.2 5.3 fusion.1
  97.5 0.0 copy-start
  97.5 123.7 %pmax.7 = f32[512]{0:T(512)S(1)} all-reduce(f32[512]{0:T(512)S(1)} %get-tuple-element.12), channel_id=1, replica_groups=mesh['seq'=4,'vocab'=64] {'vocab'}, use_global_device_ids=true, to_apply=%region_1.0 | all-reduce | flops 512 | bytes 4096 | tf_op jit(solution)/shard_map/pmax | solution.py:16
  221.2 0.0 all-gather.5.cloned.1.call-done
  221.2 0.0 copy-start.1
  221.2 5.4 fusion.2
  226.6 0.0 copy-done
  226.6 0.0 copy-done.1
  226.6 7.0 %fusion = (f32[512]{0:T(512)S(1)}, f32[512]{0:T(512)S(1)}, f32[512,1188]{0,1:T(8,128)}) fusion(f32[512,1188]{0,1:T(8,128)S(1)} %get-tuple-element.13, f32[512]{0:T(512)S(1)} %pmax.7, f32[512,1188]{0,1:T(8,128)S(1)} %fusion.2, bf16[512,2048]{0,1:T(8,128)(2,1)S(1)} %copy-done.1, bf16[2048,1188]{0,1:T(8,128)(2,1)} %param.7), kind=kOutput, calls=%fused_computation.6 | convolution fusion | flops 2494456832 | bytes 14268416 | tf_op jit(solution)/shard_map/dot_general | solution.py:13
  233.6 126.8 %all-reduce = (f32[512,1]{0,1:T(1,128)S(1)}, f32[512,1]{0,1:T(1,128)S(1)}) all-reduce(f32[512,1]{0,1:T(1,128)S(1)} %bitcast.24, f32[512,1]{0,1:T(1,128)S(1)} %bitcast.23), channel_id=1, replica_groups=mesh['seq'=4,'vocab'=64] {'vocab'}, use_global_device_ids=true, to_apply=%region_5.0 | all-reduce | flops 1024 | bytes 8192 | tf_op jit(solution)/shard_map/psum | solution.py:18
  360.4 3.1 multiply_convert_fusion
  363.5 6.9 %convolution_bitcast_fusion.1 = f32[2048,512]{0,1:T(8,128)} fusion(bf16[512,1188]{0,1:T(8,128)(2,1)S(1)} %multiply_convert_fusion, bf16[2048,1188]{0,1:T(8,128)(2,1)} %param.6), kind=kOutput, calls=%fused_computation.2 | convolution fusion | flops 2491416576 | bytes 10276864 | tf_op jit(solution)/shard_map/dot_general | solution.py:24
  370.3 5.4 copy.9
  375.7 0.0 copy-start.2
  375.7 0.0 reduce-scatter.7.cloned.1.call-update
  375.7 0.0 reduce-scatter.5.cloned.1.call-start
  375.8 1.5 copy-done.2
  377.3 5.2 convolution_bitcast_fusion
  382.5 0.0 reduce-scatter.5.cloned.1.call-update
  382.5 129.3 %reduce-scatter.7.cloned.1.call-done = f32[32,512]{1,0:T(8,128)} async-done(((f32[2048,512]{1,0:T(8,128)}), f32[32,512]{1,0:T(8,128)}) %reduce-scatter.7.cloned.1.call-update) | async-done | bytes 65552
  511.9 101.0 %reduce-scatter.5.cloned.1.call-done = f32[512,1188]{0,1:T(8,128)} async-done(((f32[2048,1188]{0,1:T(8,128)}), f32[512,1188]{0,1:T(8,128)}) %reduce-scatter.5.cloned.1.call-update) | async-done | bytes 2433040 | tf_op jit(solution)/shard_map/reduce_scatter | solution.py:32
  (1 shorter events, 0.0 us)
Async XLA Ops:
  7.2 85.0 %all-gather.3.cloned.1.call-start = ((), (), s32[]{:S(2)}) async-start(), calls=%async_computation.2 | async-start | bytes 2129920 | tf_op jit(solution)/shard_map/all_gather | solution.py:9
  7.9 213.3 %all-gather.5.cloned.1.call-start = ((), (), s32[]{:S(2)}) async-start(), calls=%async_computation.3 | async-start | bytes 2129920 | tf_op jit(solution)/shard_map/all_gather | solution.py:10
  8.6 503.2 %reduce-scatter.7.cloned.1.call-start = ((), (), s32[]{:S(2)}) async-start(), calls=%async_computation.5 | async-start | bytes 4259840
  97.5 129.1 %copy-start = (f32[512,1188]{0,1:T(8,128)}, f32[512,1188]{0,1:T(8,128)S(1)}, u32[]{:S(2)}) copy-start(f32[512,1188]{0,1:T(8,128)S(1)} %get-tuple-element.13) | copy-start | bytes 7299076
  221.2 5.4 copy-start.1
  375.7 1.6 copy-start.2
  375.7 237.1 %reduce-scatter.5.cloned.1.call-start = ((), (), s32[]{:S(2)}) async-start(), calls=%async_computation.4 | async-start | bytes 12206080 | tf_op jit(solution)/shard_map/reduce_scatter | solution.py:32
Sparse Core Ops, SparseCore 0:
  10.8 81.3 all-gather.2
  95.0 74.9 all-gather.4
  375.9 135.9 reduce-scatter.6
  515.1 97.6 reduce-scatter.4
where the time goes:
time: 620 us; the launch traced here: 619 us
  waiting for transfers between devices  315 us (51%)
  blocking collectives  250 us (40%)
  matrix products  29.7 us (5%)
  between operations  13.8 us (2%)
  local copies, waits for them, and re-layouts  6.92 us (1%)
    unnamed x5, waiting for transfers between devices  131 us
    psum x1, blocking collectives, per_device(): lax.psum((jnp.sum(scaled, axis=1, keepdims=True), jnp.sum(scaled * moved,...  127 us
    pmax x1, blocking collectives, per_device(): top = lax.pmax(jnp.max(logits, axis=1, keepdims=True), 'vocab')  124 us
    reduce_scatter x1, waiting for transfers between devices, per_device(): lax.psum_scatter(lax.dot_general(full_hidden, probe, (((0,), (0,)), ((),...  101 us
    all_gather x1, waiting for transfers between devices, per_device(): lax.all_gather(hidden, 'vocab', axis=1, tiled=True)  83.5 us
  transfers between devices with their start and end apart: 4, of which 3 were waited for; matrix products, arithmetic and copies ran while one was open for 2% of the time, Pallas kernels for 0%

commit v1 on v0

v1 whole, which is shorter than its diff:
```python
import jax
import jax.numpy as jnp
from jax import lax
from jax.experimental import pallas as pl
from jax.experimental.pallas import tpu as pltpu
from jax.sharding import PartitionSpec as P

NZ, NX, NC, NY = 8, 4, 2, 4
F32, BF16 = jnp.float32, jnp.bfloat16
BLOCK = 400
HALF = 608
SMEM = pl.BlockSpec(memory_space=pltpu.SMEM)
VMEM = pl.BlockSpec(memory_space=pltpu.VMEM)


def params(mib):
    return pltpu.CompilerParams(vmem_limit_bytes=mib * 2**20)


def receive(a, pair=0, quad=0, x=0, core=0):
    perm = []
    for i in range(NZ * NX * NC):
        q, p, xx, c = i // 16, i // 8 % 2, i // 2 % 4, i % 2
        src = (((q + quad) % 4 * 2 + (p + pair) % 2) * NX + (xx + x) % NX) * NC + (c + core) % NC
        perm.append((src, i))
    return lax.ppermute(a, "vocab", perm)


def seq_shift(a, k):
    return lax.ppermute(a, "seq", [((y + k) % NY, y) for y in range(NY)])


def stack_kernel(*refs):
    *parts, out = refs
    for k, part in enumerate(parts):
        out[k] = part[...]


def stack(parts):
    out = (len(parts),) + parts[0].shape
    return pl.pallas_call(
        stack_kernel,
        in_specs=[VMEM] * len(parts),
        out_specs=VMEM,
        out_shape=jax.ShapeDtypeStruct(out, parts[0].dtype),
        compiler_params=params(4),
        cost_estimate=pl.CostEstimate(flops=0, bytes_accessed=4 * len(parts) * parts[0].size, transcendentals=0),
    )(*parts)


def fill(out, pos_ref, own, other):
    x, c = pos_ref[0], pos_ref[1]
    for src, cc in ((own, c), (other, 1 - c)):
        for kx in range(NX):
            for zz in range(NZ):
                row = zz * 256 + lax.rem(x + kx, NX) * 64 + cc * 32
                out[pl.ds(pl.multiple_of(row, 32), 32), :] = src[kx, zz]


def pick_kernel(pos_ref, own, *outs):
    x, y = pos_ref[0], pos_ref[2]
    for k, out in enumerate(outs):
        place = lax.rem(y + k + 1, NY) * (NZ // NY)
        for kx in range(NX):
            for j in range(NZ // NY):
                row = j * 128 + lax.rem(x + kx, NX) * 32
                out[pl.ds(pl.multiple_of(row, 32), 32), :] = own[kx, place + j]


def pick(pos, own):
    tok = own.shape[-1]
    return pl.pallas_call(
        pick_kernel,
        in_specs=[SMEM, VMEM],
        out_specs=[VMEM] * (NY - 1),
        out_shape=[jax.ShapeDtypeStruct((NZ * 128 // NY, tok), BF16)] * (NY - 1),
        compiler_params=params(8),
        cost_estimate=pl.CostEstimate(flops=0, bytes_accessed=2 * 2**20, transcendentals=0),
    )(pos, own)


def first_kernel(pos_ref, own, other, w_ref, d_ref, l_ref, m_ref, mine_ref, h_ref):
    @pl.when(pl.program_id(0) == 0)
    def _():
        fill(h_ref, pos_ref, own, other)
        part = mine_ref.shape[0]
        mine_ref[...] = h_ref[pl.ds(pl.multiple_of(pos_ref[2] * part, part), part), :]

    h = h_ref[...]
    l_ref[...] = jnp.dot(w_ref[...], h, preferred_element_type=F32)
    m_ref[...] = jnp.dot(d_ref[...], h, preferred_element_type=F32)


def first(pos, own, other, w, d):
    n, k = w.shape
    tok = own.shape[-1]
    whole = pl.BlockSpec(own.shape, lambda i: (0, 0, 0, 0))
    part = pl.BlockSpec((BLOCK, k), lambda i: (i, 0))
    res = pl.BlockSpec((BLOCK, tok), lambda i: (i, 0))
    return pl.pallas_call(
        first_kernel,
        grid=(pl.cdiv(n, BLOCK),),
        in_specs=[SMEM, whole, whole, part, part],
        out_specs=[res, res, pl.BlockSpec((k // NY, tok), lambda i: (0, 0))],
        out_shape=[jax.ShapeDtypeStruct((n, tok), F32)] * 2 + [jax.ShapeDtypeStruct((k // NY, tok), BF16)],
        scratch_shapes=[pltpu.VMEM((k, tok), BF16)],
        compiler_params=params(48),
        cost_estimate=pl.CostEstimate(
            flops=4 * n * k * tok, bytes_accessed=4 * n * k + 8 * n * tok, transcendentals=0
        ),
    )(pos, own, other, w, d)


def second_kernel(n, pos_ref, own, other, w_ref, l_ref, p_ref, m_ref, o_ref, t_ref, s_ref):
    i = pl.program_id(0)
    tok = t_ref.shape[1]

    @pl.when(i == 0)
    def _():
        fill(t_ref, pos_ref, own, other)
        s_ref[0:1, :] = jnp.full((1, tok), -jnp.inf, F32)
        s_ref[1:8, :] = jnp.zeros((7, tok), F32)

    moved = jnp.dot(w_ref[...], t_ref[...], preferred_element_type=F32) + p_ref[...]
    m_ref[...] = moved
    row = lax.broadcasted_iota(jnp.int32, moved.shape, 0) + i * BLOCK
    logits = jnp.where(row < n, l_ref[...], -jnp.inf)
    moved = jnp.where(row < n, moved, 0.0)
    old = s_ref[0:1, :]
    top = jnp.maximum(old, jnp.max(logits, axis=0, keepdims=True))
    e = jnp.exp(logits - top)
    scale = jnp.exp(old - top)
    s_ref[0:1, :] = top
    s_ref[1:2, :] = s_ref[1:2, :] * scale + jnp.sum(e, axis=0, keepdims=True)
    s_ref[2:3, :] = s_ref[2:3, :] * scale + jnp.sum(e * moved, axis=0, keepdims=True)

    @pl.when(i == pl.num_programs(0) - 1)
    def _():
        for k in range(o_ref.shape[0]):
            o_ref[k] = s_ref[0:3, :]


def second(pos, own, other, w, logits, partial):
    n, k = w.shape
    tok = own.shape[-1]
    whole = pl.BlockSpec(own.shape, lambda i: (0, 0, 0, 0))
    res = pl.BlockSpec((BLOCK, tok), lambda i: (i, 0))
    return pl.pallas_call(
        lambda *refs: second_kernel(n, *refs),
        grid=(pl.cdiv(n, BLOCK),),
        in_specs=[SMEM, whole, whole, pl.BlockSpec((BLOCK, k), lambda i: (i, 0)), res, res],
        out_specs=[res, pl.BlockSpec((8, 3, tok), lambda i: (0, 0, 0))],
        out_shape=[jax.ShapeDtypeStruct((n, tok), F32), jax.ShapeDtypeStruct((8, 3, tok), F32)],
        scratch_shapes=[pltpu.VMEM((k, tok), BF16), pltpu.VMEM((8, tok), F32)],
        compiler_params=params(24),
        cost_estimate=pl.CostEstimate(
            flops=2 * n * k * tok, bytes_accessed=2 * n * k + 12 * n * tok, transcendentals=n * tok
        ),
    )(pos, own, other, w, logits, partial)


def merged(s_ref):
    tops = s_ref[:, 0, :]
    top = jnp.max(tops, axis=0, keepdims=True)
    scale = jnp.exp(tops - top)
    total = jnp.sum(s_ref[:, 1, :] * scale, axis=0, keepdims=True)
    return top, total, jnp.sum(s_ref[:, 2, :] * scale, axis=0, keepdims=True)


def merge_kernel(s_ref, o_ref):
    for at, value in enumerate(merged(s_ref)):
        for k in range(o_ref.shape[0]):
            o_ref[k, at : at + 1, :] = value


def merge(stats):
    return pl.pallas_call(
        merge_kernel,
        in_specs=[VMEM],
        out_specs=VMEM,
        out_shape=jax.ShapeDtypeStruct(stats.shape, F32),
        compiler_params=params(4),
    )(stats)


def probe_kernel(s_ref, l_ref, m_ref, p_ref, k_ref):
    @pl.when(pl.program_id(0) == 0)
    def _():
        top, total, weighted = merged(s_ref)
        k_ref[0:1, :] = top
        k_ref[1:2, :] = 1.0 / total
        k_ref[2:3, :] = weighted / total

    p_ref[...] = (jnp.exp(l_ref[...] - k_ref[0:1, :]) * k_ref[1:2, :] * (m_ref[...] - k_ref[2:3, :])).astype(BF16)


def probe_of(stats, logits, moved):
    n, tok = logits.shape
    part = pl.BlockSpec((BLOCK, tok), lambda i: (i, 0))
    return pl.pallas_call(
        probe_kernel,
        grid=(pl.cdiv(n, BLOCK),),
        in_specs=[pl.BlockSpec(stats.shape, lambda i: (0, 0, 0)), part, part],
        out_specs=part,
        out_shape=jax.ShapeDtypeStruct((n, tok), BF16),
        scratch_shapes=[pltpu.VMEM((8, tok), F32)],
        compiler_params=params(16),
        cost_estimate=pl.CostEstimate(flops=4 * n * tok, bytes_accessed=10 * n * tok, transcendentals=n * tok),
    )(stats, logits, moved)


def turn_kernel(up, down, own, other, x1, x2, x3, far_a, far_b, keep, away):
    far_a[...] = up[0:HALF, :]
    far_b[...] = down[HALF:, :]
    for z in range(NZ):
        total = own[z] + other[0, z]
        for part in (x1, x2, x3):
            total += part[z].astype(F32)
        if z < NZ // 2:
            keep[z] = total
        else:
            away[z - NZ // 2] = total


def turn(up, down, own, other, from_x):
    n, tok = up.shape
    half = (NZ // 2,) + own.shape[1:]
    return pl.pallas_call(
        turn_kernel,
        in_specs=[VMEM] * 7,
        out_specs=[VMEM] * 4,
        out_shape=[
            jax.ShapeDtypeStruct((HALF, tok), BF16),
            jax.ShapeDtypeStruct((n - HALF, tok), BF16),
            jax.ShapeDtypeStruct(half, F32),
            jax.ShapeDtypeStruct(half, F32),
        ],
        compiler_params=params(8),
        cost_estimate=pl.CostEstimate(flops=0, bytes_accessed=4 * n * tok, transcendentals=0),
    )(up, down, own, other, *from_x)


NT = (((1,), (1,)), ((), ()))


def near_kernel(pos_ref, probe, up, down, mine, r_down, r_far, r_up, q, acc, far, h_ref):
    c = pos_ref[1]
    for k, (own, out) in enumerate(((r_down, h_ref.at[0]), (r_far, far), (r_up, h_ref.at[1]))):
        for i in range(own.shape[0] // 32):
            lo, hi = i * 32, i * 32 + 32
            out[pl.ds(pl.multiple_of(lo * 2 + c * 32, 32), 32), :] = own[lo:hi, :]
            out[pl.ds(pl.multiple_of(lo * 2 + (1 - c) * 32, 32), 32), :] = q[k, lo:hi, :]
    for lo, hi in ((0, HALF), (HALF, acc.shape[0])):
        total = lax.dot_general(probe[lo:hi, :], mine[...], NT, preferred_element_type=F32)
        total += lax.dot_general(down[lo:hi, :], h_ref[0], NT, preferred_element_type=F32)
        acc[lo:hi, :] = total + lax.dot_general(up[lo:hi, :], h_ref[1], NT, preferred_element_type=F32)


def near_weight(pos, probes, mine, received, swapped):
    n = probes[0].shape[0]
    part, tok = mine.shape
    return pl.pallas_call(
        near_kernel,
        in_specs=[SMEM] + [VMEM] * 8,
        out_specs=[VMEM] * 2,
        out_shape=[jax.ShapeDtypeStruct((n, part), F32), jax.ShapeDtypeStruct((part, tok), BF16)],
        scratch_shapes=[pltpu.VMEM((2, part, tok), BF16)],
        compiler_params=params(20),
        cost_estimate=pl.CostEstimate(flops=6 * n * part * tok, bytes_accessed=10 * n * part, transcendentals=0),
    )(pos, *probes, mine, *received, swapped)


def far_kernel(acc, far_a, far_b, hidden, out):
    out[0:HALF, :] = acc[0:HALF, :] + lax.dot_general(far_a[...], hidden[...], NT, preferred_element_type=F32)
    out[HALF:, :] = acc[HALF:, :] + lax.dot_general(far_b[...], hidden[...], NT, preferred_element_type=F32)


def far_weight(acc, far_a, far_b, hidden):
    n, part = acc.shape
    return pl.pallas_call(
        far_kernel,
        in_specs=[VMEM] * 4,
        out_specs=VMEM,
        out_shape=jax.ShapeDtypeStruct((n, part), F32),
        compiler_params=params(16),
        cost_estimate=pl.CostEstimate(flops=2 * n * part * part, bytes_accessed=10 * n * part, transcendentals=0),
    )(acc, far_a, far_b, hidden)


def rows_kernel(pos_ref, p_ref, w_ref, own_ref, rest_ref, *refs):
    *other, res_ref = refs
    x, c = pos_ref[0], pos_ref[1]
    res_ref[...] = lax.dot_general(w_ref[...], p_ref[...], (((0,), (0,)), ((), ())), preferred_element_type=F32)
    each = NX // len(other)
    for kx in range(NX):
        row = lax.rem(x + kx, NX) * 64
        out, at = (rest_ref, kx - 1) if kx else (own_ref, 0)
        out[at, 0] = res_ref[pl.ds(pl.multiple_of(row + c * 32, 32), 32), :]
        out = other[kx // each]
        out[kx % each, 0] = res_ref[pl.ds(pl.multiple_of(row + (1 - c) * 32, 32), 32), :]


def rows(pos, p, w):
    n, dim = w.shape
    tok = p.shape[1]
    per = dim // NZ
    counts = [1, NX - 1, NX // 2, NX // 2]

    def z_block(i, pos_ref):
        z = pos_ref[3]
        return (0, lax.rem(z // 2 + i % 4, 4) * 2 + lax.rem(z % 2 + i // 4, 2))

    return pl.pallas_call(
        rows_kernel,
        grid_spec=pltpu.PrefetchScalarGridSpec(
            num_scalar_prefetch=1,
            grid=(NZ,),
            in_specs=[
                pl.BlockSpec(p.shape, lambda i, pos_ref: (0, 0)),
                pl.BlockSpec((n, per), z_block),
            ],
            out_specs=[pl.BlockSpec((m, 1, 32, tok), lambda i, pos_ref: (0, i, 0, 0)) for m in counts],
            scratch_shapes=[pltpu.VMEM((per, tok), F32)],
        ),
        out_shape=[jax.ShapeDtypeStruct((m, NZ, 32, tok), F32) for m in counts],
        compiler_params=params(16),
        cost_estimate=pl.CostEstimate(
            flops=2 * n * dim * tok, bytes_accessed=2 * n * dim + 4 * dim * tok, transcendentals=0
        ),
    )(pos, p, w)


Z_GROUPS = [[(z * NX + x) * NC + c for z in range(NZ)] for x in range(NX) for c in range(NC)]

XC_GROUPS = [[z * NX * NC + i for i in range(NX * NC)] for z in range(NZ)]


def exchange(a, groups):
    return lax.all_to_all(a, "vocab", 0, 0, axis_index_groups=groups, tiled=True)


def per_device(hidden, tangent, head_weight, weight_dir):
    v = lax.axis_index("vocab")
    y = lax.axis_index("seq")
    pos = jnp.stack([(v // NC) % NX, v % NC, y, v // (NX * NC)]).astype(jnp.int32)
    w, wd = head_weight.T, weight_dir.T

    both = jnp.stack([hidden.T, tangent.T])
    both = exchange(jnp.broadcast_to(both[None], (NZ,) + both.shape), Z_GROUPS)
    a, b = both[:, 0], both[:, 1]
    a = [a] + [receive(a, x=k) for k in range(1, NX)]
    b = [b] + [receive(b, x=k) for k in range(1, NX)]
    a0 = stack(a)
    a1 = receive(a0, core=1)
    to_up, to_far, to_down = pick(pos, a0)
    r_down, r_up = seq_shift(to_up, -1), seq_shift(to_down, 1)
    logits, partial, mine = first(pos, a0, a1, w, wd)
    partial, b, r_down, r_up, to_far = lax.optimization_barrier((partial, b, r_down, r_up, to_far))
    b0 = stack(b)
    b1 = receive(b0, core=1)
    r_far = seq_shift(to_far, 2)
    moved, stats = second(pos, b0, b1, w, logits, partial)
    stats, r_far = lax.optimization_barrier((stats, r_far))
    swapped = receive(stack([r_down, r_far, r_up]), core=1)
    stats = merge(exchange(stats, XC_GROUPS))
    stats, swapped = lax.optimization_barrier((stats, swapped))
    stats = exchange(stats, Z_GROUPS)
    probe = probe_of(stats, logits, moved)

    up, down = seq_shift(probe, 1), seq_shift(probe, -1)
    own, rest, *other = rows(pos, probe, w)
    other = [receive(o, core=1) for o in other]
    from_x = []
    for k in range(1, NX):
        part = rest[k - 1] + other[k // 2][k % 2]
        from_x.append(receive(part.astype(BF16), x=-k))
    far_a, far_b, gh, away = turn(up, down, own[0], other[0], from_x)
    far_a, far_b = seq_shift(far_a, 1), seq_shift(far_b, -1)
    gh = gh + receive(away, pair=1)
    gh = gh[0] + sum(receive(gh[k], quad=-k) for k in range(1, 4))
    acc, far = near_weight(pos, [probe, up, down], mine, [r_down, r_far, r_up], swapped)
    gw = far_weight(acc, far_a, far_b, far)
    return gh.T, gw.T


def solution(mesh):
    placed = (P("seq", "vocab"), P("seq", "vocab"), P(None, "vocab"), P(None, "vocab"))
    return jax.shard_map(
        per_device,
        mesh=mesh,
        in_specs=placed,
        out_specs=(P("seq", "vocab"), P("seq", "vocab")),
        check_vma=False,
    )
```

time: 620 us -> 150 us (0.24)
  waiting for transfers between devices: 315 us -> 40.7 us
  blocking collectives: 250 us -> 41.7 us
  starting transfers between devices: 0.16 us -> 34 us
  matrix products: 29.7 us -> 0 us
  Pallas kernels: 0 us -> 27.3 us
  between operations: 13.8 us -> 0.79 us
    unnamed x5 -> x0, waiting for transfers between devices: 131 us -> none
    psum x1 -> x0, blocking collectives: 127 us -> none  [per_device(): lax.psum((jnp.sum(scaled, axis=1, keepdims=True), jnp.sum(scaled * moved,...]
    pmax x1 -> x0, blocking collectives: 124 us -> none  [per_device(): top = lax.pmax(jnp.max(logits, axis=1, keepdims=True), 'vocab')]
    reduce_scatter x1 -> x0, waiting for transfers between devices: 101 us -> none  [per_device(): lax.psum_scatter(lax.dot_general(full_hidden, probe, (((0,), (0,)), ((),...]
    all_gather x2 -> x0, waiting for transfers between devices: 83.5 us -> none  [the longest x1 83.5 us: per_device(): lax.all_gather(hidden, 'vocab', axis=1, tiled=True)]
    all_to_all x0 -> x3, blocking collectives: none -> 41.7 us  [exchange(): lax.all_to_all(a, 'vocab', 0, 0, axis_index_groups=groups, tiled=True)]
    ppermute x0 -> x25, waiting for transfers between devices: none -> 40.7 us  [the longest x7 23.9 us: seq_shift(): return lax.ppermute(a, 'seq', [((y + k) % NY, y) for y in range(NY)])]
    ppermute x0 -> x25, starting transfers between devices: none -> 34 us  [the longest x18 24 us: receive(): return lax.ppermute(a, 'vocab', perm)]
  transfers between devices with their start and end apart: 4 -> 25, of which waited for: 3 -> 10; matrix products, arithmetic and copies ran while one was open for 2% -> 1% of each run, Pallas kernels for 0% -> 12%
where the time goes in v1:
time: 150 us; the launch traced here: 148 us
  blocking collectives  41.7 us (28%)
  waiting for transfers between devices  40.7 us (27%)
  starting transfers between devices  34 us (23%)
  Pallas kernels  27.3 us (18%)
  other arithmetic  1.96 us (1%)
  local copies, waits for them, and re-layouts  1.79 us (1%)
    all_to_all x3, blocking collectives, exchange(): lax.all_to_all(a, 'vocab', 0, 0, axis_index_groups=groups, tiled=True)  41.7 us
    ppermute x18, starting transfers between devices, receive(): return lax.ppermute(a, 'vocab', perm)  24 us
    ppermute x7, waiting for transfers between devices, seq_shift(): return lax.ppermute(a, 'seq', [((y + k) % NY, y) for y in range(NY)])  23.9 us
    ppermute x18, waiting for transfers between devices, receive(): return lax.ppermute(a, 'vocab', perm)  16.8 us
    ppermute x7, starting transfers between devices, seq_shift(): return lax.ppermute(a, 'seq', [((y + k) % NY, y) for y in range(NY)])  9.98 us
    pallas_call x1, Pallas kernels, first(): pl.pallas_call(first_kernel, grid=(pl.cdiv(n, BLOCK),), in_specs=[SMEM, w...  9.24 us
    pallas_call x1, Pallas kernels, rows(): pl.pallas_call(rows_kernel, grid_spec=pltpu.PrefetchScalarGridSpec(num_sc...  6.57 us
    pallas_call x1, Pallas kernels, second(): pl.pallas_call(lambda *refs: second_kernel(n, *refs), grid=(pl.cdiv(n, BL...  4.46 us
  transfers between devices with their start and end apart: 25, of which 10 were waited for; matrix products, arithmetic and copies ran while one was open for 1% of the time, Pallas kernels for 12%

profile of v1, /device:TPU:1, one launch (start us, length us, event | category | flops | bytes accessed | tf_op | source)
XLA Modules:
  0.0 148.3 jit_solution(2510160536772409858)
XLA Ops:
  0.6 0.8 pad_maximum_fusion
  1.5 24.8 %all_to_all.15 = bf16[8,2,32,512]{3,2,1,0:T(8,128)(2,1)S(1)} all-to-all(bf16[8,2,32,512]{3,2,1,0:T(8,128)(2,1)S(1)} %broadcast_in_dim.2), channel_id=1, replica_groups={{0,8,16,24,32,40,48,56},{1,9,17,25,33,41,49,57},{2,10,18,26,34,42,50,58..., dimensions={0} | all-to-all | bytes 1048576 | tf_op jit(solution)/shard_map/all_to_all | solution.py:339
  26.3 1.3 collective-permute-start.2
  27.6 2.5 %collective-permute-start.1 = (bf16[8,32,512]{2,1,0:T(8,128)(2,1)S(1)}, bf16[8,32,512]{2,1,0:T(8,128)(2,1)S(1)}, u32[]{:S(2)}, u32[]{:S(2)}) collective-permute-start(bf16[8,32,512]{2,1,0:T(8,128)(2,1)S(1)} %get-tuple-element.66.refs_0_), channel_id=1, source_target_pairs={{4,0},{5,1},{6,2},{7,3},{0,4},{1,5},{2,6},{3,7},{12,8},{13,9},{14,... | collective-permute-start | bytes 786440 | tf_op jit(solution)/shard_map/ppermute | solution.py:26
  30.0 1.2 collective-permute-start
  31.2 1.6 %collective-permute-done.2.refs_3_ = bf16[8,32,512]{2,1,0:T(8,128)(2,1)S(1)} collective-permute-done((bf16[8,32,512]{2,1,0:T(8,128)(2,1)S(1)}, bf16[8,32,512]{2,1,0:T(8,128)(2,1)S(1)}, u32[]{:S(2)}, u32[]{:S(2)}) %collective-permute-start.2) | collective-permute-done | bytes 262176 | tf_op jit(solution)/shard_map/ppermute | solution.py:26
  32.8 6.4 %collective-permute-done.1.refs_2_ = bf16[8,32,512]{2,1,0:T(8,128)(2,1)S(1)} collective-permute-done((bf16[8,32,512]{2,1,0:T(8,128)(2,1)S(1)}, bf16[8,32,512]{2,1,0:T(8,128)(2,1)S(1)}, u32[]{:S(2)}, u32[]{:S(2)}) %collective-permute-start.1) | collective-permute-done | bytes 262176 | tf_op jit(solution)/shard_map/ppermute | solution.py:26
  39.2 0.2 collective-permute-done.refs_1_
  39.5 3.6 %collective-permute-start.3 = (bf16[4,8,32,512]{3,2,1,0:T(8,128)(2,1)S(1)}, bf16[4,8,32,512]{3,2,1,0:T(8,128)(2,1)S(1)}, u32[]{:S(2)}, u32[]{:S(2)}) collective-permute-start(bf16[4,8,32,512]{3,2,1,0:T(8,128)(2,1)S(1)} %shard_map.59.own), channel_id=1, source_target_pairs={{1,0},{0,1},{3,2},{2,3},{5,4},{4,5},{7,6},{6,7},{9,8},{8,9},{11,10... | collective-permute-start | bytes 3145736 | tf_op jit(solution)/shard_map/ppermute | solution.py:26
  43.2 1.1 collective-permute-start.6
  44.2 2.1 %collective-permute-start.5 = (bf16[8,32,512]{2,1,0:T(8,128)(2,1)S(1)}, bf16[8,32,512]{2,1,0:T(8,128)(2,1)S(1)}, u32[]{:S(2)}, u32[]{:S(2)}) collective-permute-start(bf16[8,32,512]{2,1,0:T(8,128)(2,1)S(1)} %get-tuple-element.36.refs_0_), channel_id=1, source_target_pairs={{4,0},{5,1},{6,2},{7,3},{0,4},{1,5},{2,6},{3,7},{12,8},{13,9},{14,... | collective-permute-start | bytes 786440 | tf_op jit(solution)/shard_map/ppermute | solution.py:26
  46.3 1.3 collective-permute-start.4
  47.6 0.6 shard_map.61
  48.2 1.4 collective-permute-start.7
  49.6 1.5 %collective-permute-start.8 = (bf16[256,512]{1,0:T(8,128)(2,1)S(1)}, bf16[256,512]{1,0:T(8,128)(2,1)S(1)}, u32[]{:S(2)}, u32[]{:S(2)}) collective-permute-start(bf16[256,512]{1,0:T(8,128)(2,1)S(1)} %get-tuple-element.34), channel_id=1, source_target_pairs={{64,0},{128,64},{192,128},{0,192},{65,1},{129,65},{193,129},{1,193... | collective-permute-start | bytes 786440 | tf_op jit(solution)/shard_map/ppermute | solution.py:30
  51.2 9.2 %shard_map.60 = (f32[1188,512]{1,0:T(8,128)S(1)}, f32[1188,512]{1,0:T(8,128)}, bf16[512,512]{1,0:T(8,128)(2,1)S(1)}) custom-call(s32[4]{0:T(128)S(1)} %pad_add_fusion.pos_ref.refs_0_, bf16[4,8,32,512]{3,2,1,0:T(8,128)(2,1)S(1)} %shard_map.59.own, bf16[4,8,32,512]{3,2,1,0:T(8,128)(2,1)S(1)} %collective-permute-done.3.other, bf16[1188,2048]{1,0:T(8,128)(2,1)} %bitcast.42, ...), custom_call_target="tpu_custom_call" | custom-call | flops 4982833152 | bytes 14598144 | tf_op jit(solution)/shard_map/pallas_call | solution.py:100
  60.5 1.4 collective-permute-start.9
  61.9 1.7 %collective-permute-start.10 = (bf16[256,512]{1,0:T(8,128)(2,1)S(1)}, bf16[256,512]{1,0:T(8,128)(2,1)S(1)}, u32[]{:S(2)}, u32[]{:S(2)}) collective-permute-start(bf16[256,512]{1,0:T(8,128)(2,1)S(1)} %get-tuple-element.43), channel_id=1, source_target_pairs={{128,0},{192,64},{0,128},{64,192},{129,1},{193,65},{1,129},{65,193... | collective-permute-start | bytes 786440 | tf_op jit(solution)/shard_map/ppermute | solution.py:30
  63.6 0.6 collective-permute-done.9.refs_2_
  64.2 1.7 %copy-done = f32[1188,512]{1,0:T(8,128)S(1)} copy-done((f32[1188,512]{1,0:T(8,128)S(1)}, f32[1188,512]{1,0:T(8,128)}, u32[]{:S(2)}) %copy-start) | copy-done | bytes 2433048
  65.9 4.5 %shard_map.63 = (f32[1188,512]{1,0:T(8,128)S(1)}, f32[8,3,512]{2,1,0:T(4,128)S(1)}) custom-call(s32[4]{0:T(128)S(1)} %pad_add_fusion.pos_ref.refs_0_, bf16[4,8,32,512]{3,2,1,0:T(8,128)(2,1)S(1)} %shard_map.62.refs_1_, bf16[4,8,32,512]{3,2,1,0:T(8,128)(2,1)S(1)} %collective-permute-done.9.refs_2_, bf16[1188,2048]{1,0:T(8,128)(2,1)S(1)} %bitcast.45, ...), custom_call_target="tpu_custom_call" | custom-call | flops 2491416576 | bytes 12165120 | tf_op jit(solution)/shard_map/pallas_call | solution.py:148
  70.4 0.9 collective-permute-done.10.refs_1_.r_far
  71.3 1.0 collective-permute-start.11
  72.3 7.2 %all_to_all.16.s_ref = f32[8,3,512]{2,1,0:T(4,128)S(1)} all-to-all(f32[8,3,512]{2,1,0:T(4,128)S(1)} %get-tuple-element.44), channel_id=1, replica_groups={{0,1,2,3,4,5,6,7},{8,9,10,11,12,13,14,15},{16,17,18,19,20,21,22,23},{24..., dimensions={0} | all-to-all | bytes 98304 | tf_op jit(solution)/shard_map/all_to_all | solution.py:339
  79.6 9.7 %all_to_all.17.s_ref = f32[8,3,512]{2,1,0:T(4,128)S(1)} all-to-all(f32[8,3,512]{2,1,0:T(4,128)S(1)} %shard_map.64), channel_id=1, replica_groups={{0,8,16,24,32,40,48,56},{1,9,17,25,33,41,49,57},{2,10,18,26,34,42,50,58..., dimensions={0} | all-to-all | bytes 98304 | tf_op jit(solution)/shard_map/all_to_all | solution.py:339
  89.3 1.0 shard_map.66.p_ref.probe
  90.3 6.6 %shard_map.67 = (f32[1,8,32,512]{3,2,1,0:T(8,128)S(1)}, f32[3,8,32,512]{3,2,1,0:T(8,128)S(1)}, f32[2,8,32,512]{3,2,1,0:T(8,128)S(1)}, f32[2,8,32,512]{3,2,1,0:T(8,128)S(1)}) custom-call(s32[4]{0:T(128)S(1)} %pad_add_fusion.pos_ref.refs_0_, bf16[1188,512]{1,0:T(8,128)(2,1)S(1)} %shard_map.66.p_ref.probe, bf16[1188,2048]{1,0:T(8,128)(2,1)S(1)} %bitcast.46), custom_call_target="tpu_custom_call" | custom-call | flops 2491416576 | bytes 9060352 | tf_op jit(solution)/shard_map/pallas_call | solution.py:313
  96.8 2.5 %collective-permute-start.14 = (f32[2,8,32,512]{3,2,1,0:T(8,128)S(1)}, f32[2,8,32,512]{3,2,1,0:T(8,128)S(1)}, u32[]{:S(2)}, u32[]{:S(2)}) collective-permute-start(f32[2,8,32,512]{3,2,1,0:T(8,128)S(1)} %get-tuple-element.51), channel_id=1, source_target_pairs={{1,0},{0,1},{3,2},{2,3},{5,4},{4,5},{7,6},{6,7},{9,8},{8,9},{11,10... | collective-permute-start | bytes 3145736 | tf_op jit(solution)/shard_map/ppermute | solution.py:26
  99.3 0.1 collective-permute-start.16
  99.4 0.4 collective-permute-start.13
  99.8 2.3 %collective-permute-start.12 = (bf16[1188,512]{1,0:T(8,128)(2,1)S(1)}, bf16[1188,512]{1,0:T(8,128)(2,1)S(1)}, u32[]{:S(2)}, u32[]{:S(2)}) collective-permute-start(bf16[1188,512]{1,0:T(8,128)(2,1)S(1)} %shard_map.66.p_ref.probe), channel_id=1, source_target_pairs={{64,0},{128,64},{192,128},{0,192},{65,1},{129,65},{193,129},{1,193... | collective-permute-start | bytes 3649544 | tf_op jit(solution)/shard_map/ppermute | solution.py:30
  102.1 1.0 collective-permute-done.16
  103.1 0.4 fusion.5
  103.5 1.0 collective-permute-start.18
  104.5 1.2 collective-permute-start.17
  105.7 23.0 %collective-permute-done.13.down = bf16[1188,512]{1,0:T(8,128)(2,1)S(1)} collective-permute-done((bf16[1188,512]{1,0:T(8,128)(2,1)S(1)}, bf16[1188,512]{1,0:T(8,128)(2,1)S(1)}, u32[]{:S(2)}, u32[]{:S(2)}) %collective-permute-start.13) | collective-permute-done | bytes 1216544 | tf_op jit(solution)/shard_map/ppermute | solution.py:30
  128.7 0.2 shard_map.68
  128.9 0.4 collective-permute-start.19
  129.2 0.1 collective-permute-start.24
  129.4 2.6 %collective-permute-start.23 = (bf16[608,512]{1,0:T(8,128)(2,1)S(1)}, bf16[608,512]{1,0:T(8,128)(2,1)S(1)}, u32[]{:S(2)}, u32[]{:S(2)}) collective-permute-start(bf16[608,512]{1,0:T(8,128)(2,1)S(1)} %get-tuple-element.59), channel_id=1, source_target_pairs={{64,0},{128,64},{192,128},{0,192},{65,1},{129,65},{193,129},{1,193... | collective-permute-start | bytes 1867784 | tf_op jit(solution)/shard_map/ppermute | solution.py:30
  131.9 3.6 %collective-permute-done.19 = f32[4,32,512]{2,1,0:T(8,128)S(1)} collective-permute-done((f32[4,32,512]{2,1,0:T(8,128)S(1)}, f32[4,32,512]{2,1,0:T(8,128)S(1)}, u32[]{:S(2)}, u32[]{:S(2)}) %collective-permute-start.19) | collective-permute-done | bytes 262176 | tf_op jit(solution)/shard_map/ppermute | solution.py:26
  135.6 0.3 collective-permute-start.21
  135.9 3.3 %collective-permute-start.22 = (f32[32,512]{1,0:T(8,128)S(1)}, f32[32,512]{1,0:T(8,128)S(1)}, u32[]{:S(2)}, u32[]{:S(2)}) collective-permute-start(f32[32,512]{1,0:T(8,128)S(1)} %get-tuple-element.68), channel_id=1, source_target_pairs={{16,0},{17,1},{18,2},{19,3},{20,4},{21,5},{22,6},{23,7},{24,8},{25... | collective-permute-start | bytes 196616 | tf_op jit(solution)/shard_map/ppermute | solution.py:26
  139.2 2.7 %shard_map.69 = (f32[1188,512]{1,0:T(8,128)S(1)}, bf16[512,512]{1,0:T(8,128)(2,1)S(1)}) custom-call(s32[4]{0:T(128)S(1)} %pad_add_fusion.pos_ref.refs_0_, bf16[1188,512]{1,0:T(8,128)(2,1)S(1)} %shard_map.66.p_ref.probe, bf16[1188,512]{1,0:T(8,128)(2,1)S(1)} %collective-permute-done.12.up, bf16[1188,512]{1,0:T(8,128)(2,1)S(1)} %collective-permute-done.13.down, ...), custom_call_target="tpu_custom_call" | custom-call | flops 1868562432 | bytes 6082560 | tf_op jit(solution)/shard_map/pallas_call | solution.py:262
  141.9 0.8 collective-permute-done.21
  142.7 2.6 %collective-permute-done.20 = f32[32,512]{1,0:T(8,128)S(1)} collective-permute-done((f32[32,512]{1,0:T(8,128)S(1)}, f32[32,512]{1,0:T(8,128)S(1)}, u32[]{:S(2)}, u32[]{:S(2)}) %collective-permute-start.20) | collective-permute-done | bytes 65568 | tf_op jit(solution)/shard_map/ppermute | solution.py:26
  145.4 0.6 fusion.7
  146.0 2.3 %shard_map.70 = f32[1188,512]{1,0:T(8,128)} custom-call(f32[1188,512]{1,0:T(8,128)S(1)} %get-tuple-element.58.acc, bf16[608,512]{1,0:T(8,128)(2,1)S(1)} %collective-permute-done.23.far_a, bf16[580,512]{1,0:T(8,128)(2,1)S(1)} %collective-permute-done.24.far_b, bf16[512,512]{1,0:T(8,128)(2,1)S(1)} %get-tuple-element.61.hidden), custom_call_target="tpu_custom_call" | custom-call | flops 622854144 | bytes 6082560 | tf_op jit(solution)/shard_map/pallas_call | solution.py:280
  (32 shorter events, 0.5 us)
Async XLA Ops:
  26.3 6.5 %collective-permute-start.2 = (bf16[8,32,512]{2,1,0:T(8,128)(2,1)S(1)}, bf16[8,32,512]{2,1,0:T(8,128)(2,1)S(1)}, u32[]{:S(2)}, u32[]{:S(2)}) collective-permute-start(bf16[8,32,512]{2,1,0:T(8,128)(2,1)S(1)} %get-tuple-element.66.refs_0_), channel_id=1, source_target_pairs={{6,0},{7,1},{0,2},{1,3},{2,4},{3,5},{4,6},{5,7},{14,8},{15,9},{8,1... | collective-permute-start | bytes 786440 | tf_op jit(solution)/shard_map/ppermute | solution.py:26
  27.6 11.6 %collective-permute-start.1 = (bf16[8,32,512]{2,1,0:T(8,128)(2,1)S(1)}, bf16[8,32,512]{2,1,0:T(8,128)(2,1)S(1)}, u32[]{:S(2)}, u32[]{:S(2)}) collective-permute-start(bf16[8,32,512]{2,1,0:T(8,128)(2,1)S(1)} %get-tuple-element.66.refs_0_), channel_id=1, source_target_pairs={{4,0},{5,1},{6,2},{7,3},{0,4},{1,5},{2,6},{3,7},{12,8},{13,9},{14,... | collective-permute-start | bytes 786440 | tf_op jit(solution)/shard_map/ppermute | solution.py:26
  30.0 9.4 %collective-permute-start = (bf16[8,32,512]{2,1,0:T(8,128)(2,1)S(1)}, bf16[8,32,512]{2,1,0:T(8,128)(2,1)S(1)}, u32[]{:S(2)}, u32[]{:S(2)}) collective-permute-start(bf16[8,32,512]{2,1,0:T(8,128)(2,1)S(1)} %get-tuple-element.66.refs_0_), channel_id=1, source_target_pairs={{2,0},{3,1},{4,2},{5,3},{6,4},{7,5},{0,6},{1,7},{10,8},{11,9},{12,... | collective-permute-start | bytes 786440 | tf_op jit(solution)/shard_map/ppermute | solution.py:26
  39.5 10.1 %collective-permute-start.3 = (bf16[4,8,32,512]{3,2,1,0:T(8,128)(2,1)S(1)}, bf16[4,8,32,512]{3,2,1,0:T(8,128)(2,1)S(1)}, u32[]{:S(2)}, u32[]{:S(2)}) collective-permute-start(bf16[4,8,32,512]{3,2,1,0:T(8,128)(2,1)S(1)} %shard_map.59.own), channel_id=1, source_target_pairs={{1,0},{0,1},{3,2},{2,3},{5,4},{4,5},{7,6},{6,7},{9,8},{8,9},{11,10... | collective-permute-start | bytes 3145736 | tf_op jit(solution)/shard_map/ppermute | solution.py:26
  43.2 17.2 %collective-permute-start.6 = (bf16[8,32,512]{2,1,0:T(8,128)(2,1)S(1)}, bf16[8,32,512]{2,1,0:T(8,128)(2,1)S(1)}, u32[]{:S(2)}, u32[]{:S(2)}) collective-permute-start(bf16[8,32,512]{2,1,0:T(8,128)(2,1)S(1)} %get-tuple-element.36.refs_0_), channel_id=1, source_target_pairs={{6,0},{7,1},{0,2},{1,3},{2,4},{3,5},{4,6},{5,7},{14,8},{15,9},{8,1... | collective-permute-start | bytes 786440 | tf_op jit(solution)/shard_map/ppermute | solution.py:26
  44.2 16.2 %collective-permute-start.5 = (bf16[8,32,512]{2,1,0:T(8,128)(2,1)S(1)}, bf16[8,32,512]{2,1,0:T(8,128)(2,1)S(1)}, u32[]{:S(2)}, u32[]{:S(2)}) collective-permute-start(bf16[8,32,512]{2,1,0:T(8,128)(2,1)S(1)} %get-tuple-element.36.refs_0_), channel_id=1, source_target_pairs={{4,0},{5,1},{6,2},{7,3},{0,4},{1,5},{2,6},{3,7},{12,8},{13,9},{14,... | collective-permute-start | bytes 786440 | tf_op jit(solution)/shard_map/ppermute | solution.py:26
  46.3 14.1 %collective-permute-start.4 = (bf16[8,32,512]{2,1,0:T(8,128)(2,1)S(1)}, bf16[8,32,512]{2,1,0:T(8,128)(2,1)S(1)}, u32[]{:S(2)}, u32[]{:S(2)}) collective-permute-start(bf16[8,32,512]{2,1,0:T(8,128)(2,1)S(1)} %get-tuple-element.36.refs_0_), channel_id=1, source_target_pairs={{2,0},{3,1},{4,2},{5,3},{6,4},{7,5},{0,6},{1,7},{10,8},{11,9},{12,... | collective-permute-start | bytes 786440 | tf_op jit(solution)/shard_map/ppermute | solution.py:26
  48.2 12.2 %collective-permute-start.7 = (bf16[256,512]{1,0:T(8,128)(2,1)S(1)}, bf16[256,512]{1,0:T(8,128)(2,1)S(1)}, u32[]{:S(2)}, u32[]{:S(2)}) collective-permute-start(bf16[256,512]{1,0:T(8,128)(2,1)S(1)} %get-tuple-element.33), channel_id=1, source_target_pairs={{192,0},{0,64},{64,128},{128,192},{193,1},{1,65},{65,129},{129,193... | collective-permute-start | bytes 786440 | tf_op jit(solution)/shard_map/ppermute | solution.py:30
  49.6 10.8 %collective-permute-start.8 = (bf16[256,512]{1,0:T(8,128)(2,1)S(1)}, bf16[256,512]{1,0:T(8,128)(2,1)S(1)}, u32[]{:S(2)}, u32[]{:S(2)}) collective-permute-start(bf16[256,512]{1,0:T(8,128)(2,1)S(1)} %get-tuple-element.34), channel_id=1, source_target_pairs={{64,0},{128,64},{192,128},{0,192},{65,1},{129,65},{193,129},{1,193... | collective-permute-start | bytes 786440 | tf_op jit(solution)/shard_map/ppermute | solution.py:30
  51.1 13.0 %slice-start = ((s8[4882432]{0:T(1024)(128)(4,1)}), s8[4194304]{0:T(1024)(128)(4,1)S(1)}, s32[]{:S(2)}) async-start(s8[4882432]{0:T(1024)(128)(4,1)} %bitcast.43), calls=%async_computation.3 | async-start | bytes 8388608
  51.2 13.0 %slice-start.1 = ((s8[4882432]{0:T(1024)(128)(4,1)}), s8[688128]{0:T(1024)(128)(4,1)S(1)}, s32[]{:S(2)}) async-start(s8[4882432]{0:T(1024)(128)(4,1)} %bitcast.43), calls=%async_computation.4 | async-start | bytes 1376256
  60.5 3.7 %collective-permute-start.9 = (bf16[4,8,32,512]{3,2,1,0:T(8,128)(2,1)S(1)}, bf16[4,8,32,512]{3,2,1,0:T(8,128)(2,1)S(1)}, u32[]{:S(2)}, u32[]{:S(2)}) collective-permute-start(bf16[4,8,32,512]{3,2,1,0:T(8,128)(2,1)S(1)} %shard_map.62.refs_1_), channel_id=1, source_target_pairs={{1,0},{0,1},{3,2},{2,3},{5,4},{4,5},{7,6},{6,7},{9,8},{8,9},{11,10... | collective-permute-start | bytes 3145736 | tf_op jit(solution)/shard_map/ppermute | solution.py:26
  61.9 9.4 %collective-permute-start.10 = (bf16[256,512]{1,0:T(8,128)(2,1)S(1)}, bf16[256,512]{1,0:T(8,128)(2,1)S(1)}, u32[]{:S(2)}, u32[]{:S(2)}) collective-permute-start(bf16[256,512]{1,0:T(8,128)(2,1)S(1)} %get-tuple-element.43), channel_id=1, source_target_pairs={{128,0},{192,64},{0,128},{64,192},{129,1},{193,65},{1,129},{65,193... | collective-permute-start | bytes 786440 | tf_op jit(solution)/shard_map/ppermute | solution.py:30
  64.2 1.7 %copy-start = (f32[1188,512]{1,0:T(8,128)S(1)}, f32[1188,512]{1,0:T(8,128)}, u32[]{:S(2)}) copy-start(f32[1188,512]{1,0:T(8,128)} %get-tuple-element.41.refs_5_) | copy-start | bytes 7299076
  71.3 8.2 %collective-permute-start.11 = (bf16[3,256,512]{2,1,0:T(8,128)(2,1)S(1)}, bf16[3,256,512]{2,1,0:T(8,128)(2,1)S(1)}, u32[]{:S(2)}, u32[]{:S(2)}) collective-permute-start(bf16[3,256,512]{2,1,0:T(8,128)(2,1)S(1)} %shard_map.65), channel_id=1, source_target_pairs={{1,0},{0,1},{3,2},{2,3},{5,4},{4,5},{7,6},{6,7},{9,8},{8,9},{11,10... | collective-permute-start | bytes 2359304 | tf_op jit(solution)/shard_map/ppermute | solution.py:26
  96.8 5.2 %collective-permute-start.14 = (f32[2,8,32,512]{3,2,1,0:T(8,128)S(1)}, f32[2,8,32,512]{3,2,1,0:T(8,128)S(1)}, u32[]{:S(2)}, u32[]{:S(2)}) collective-permute-start(f32[2,8,32,512]{3,2,1,0:T(8,128)S(1)} %get-tuple-element.51), channel_id=1, source_target_pairs={{1,0},{0,1},{3,2},{2,3},{5,4},{4,5},{7,6},{6,7},{9,8},{8,9},{11,10... | collective-permute-start | bytes 3145736 | tf_op jit(solution)/shard_map/ppermute | solution.py:26
  99.3 3.8 %collective-permute-start.16 = (f32[2,8,32,512]{3,2,1,0:T(8,128)S(1)}, f32[2,8,32,512]{3,2,1,0:T(8,128)S(1)}, u32[]{:S(2)}, u32[]{:S(2)}) collective-permute-start(f32[2,8,32,512]{3,2,1,0:T(8,128)S(1)} %get-tuple-element.53), channel_id=1, source_target_pairs={{1,0},{0,1},{3,2},{2,3},{5,4},{4,5},{7,6},{6,7},{9,8},{8,9},{11,10... | collective-permute-start | bytes 3145736 | tf_op jit(solution)/shard_map/ppermute | solution.py:26
  99.4 29.2 %collective-permute-start.13 = (bf16[1188,512]{1,0:T(8,128)(2,1)S(1)}, bf16[1188,512]{1,0:T(8,128)(2,1)S(1)}, u32[]{:S(2)}, u32[]{:S(2)}) collective-permute-start(bf16[1188,512]{1,0:T(8,128)(2,1)S(1)} %shard_map.66.p_ref.probe), channel_id=1, source_target_pairs={{192,0},{0,64},{64,128},{128,192},{193,1},{1,65},{65,129},{129,193... | collective-permute-start | bytes 3649544 | tf_op jit(solution)/shard_map/ppermute | solution.py:30
  99.8 28.9 %collective-permute-start.12 = (bf16[1188,512]{1,0:T(8,128)(2,1)S(1)}, bf16[1188,512]{1,0:T(8,128)(2,1)S(1)}, u32[]{:S(2)}, u32[]{:S(2)}) collective-permute-start(bf16[1188,512]{1,0:T(8,128)(2,1)S(1)} %shard_map.66.p_ref.probe), channel_id=1, source_target_pairs={{64,0},{128,64},{192,128},{0,192},{65,1},{129,65},{193,129},{1,193... | collective-permute-start | bytes 3649544 | tf_op jit(solution)/shard_map/ppermute | solution.py:30
  103.5 25.1 %collective-permute-start.18 = (bf16[8,32,512]{2,1,0:T(8,128)(2,1)S(1)}, bf16[8,32,512]{2,1,0:T(8,128)(2,1)S(1)}, u32[]{:S(2)}, u32[]{:S(2)}) collective-permute-start(bf16[8,32,512]{2,1,0:T(8,128)(2,1)S(1)} %get-tuple-element.62), channel_id=1, source_target_pairs={{2,0},{3,1},{4,2},{5,3},{6,4},{7,5},{0,6},{1,7},{10,8},{11,9},{12,... | collective-permute-start | bytes 786440 | tf_op jit(solution)/shard_map/ppermute | solution.py:26
  104.5 24.2 %collective-permute-start.17 = (bf16[8,32,512]{2,1,0:T(8,128)(2,1)S(1)}, bf16[8,32,512]{2,1,0:T(8,128)(2,1)S(1)}, u32[]{:S(2)}, u32[]{:S(2)}) collective-permute-start(bf16[8,32,512]{2,1,0:T(8,128)(2,1)S(1)} %get-tuple-element.63), channel_id=1, source_target_pairs={{4,0},{5,1},{6,2},{7,3},{0,4},{1,5},{2,6},{3,7},{12,8},{13,9},{14,... | collective-permute-start | bytes 786440 | tf_op jit(solution)/shard_map/ppermute | solution.py:26
  105.7 23.0 %collective-permute-start.15 = (bf16[8,32,512]{2,1,0:T(8,128)(2,1)S(1)}, bf16[8,32,512]{2,1,0:T(8,128)(2,1)S(1)}, u32[]{:S(2)}, u32[]{:S(2)}) collective-permute-start(bf16[8,32,512]{2,1,0:T(8,128)(2,1)S(1)} %get-tuple-element.64), channel_id=1, source_target_pairs={{6,0},{7,1},{0,2},{1,3},{2,4},{3,5},{4,6},{5,7},{14,8},{15,9},{8,1... | collective-permute-start | bytes 786440 | tf_op jit(solution)/shard_map/ppermute | solution.py:26
  128.9 6.6 %collective-permute-start.19 = (f32[4,32,512]{2,1,0:T(8,128)S(1)}, f32[4,32,512]{2,1,0:T(8,128)S(1)}, u32[]{:S(2)}, u32[]{:S(2)}) collective-permute-start(f32[4,32,512]{2,1,0:T(8,128)S(1)} %get-tuple-element.55), channel_id=1, source_target_pairs={{8,0},{9,1},{10,2},{11,3},{12,4},{13,5},{14,6},{15,7},{0,8},{1,9},... | collective-permute-start | bytes 786440 | tf_op jit(solution)/shard_map/ppermute | solution.py:26
  129.2 16.8 %collective-permute-start.24 = (bf16[580,512]{1,0:T(8,128)(2,1)S(1)}, bf16[580,512]{1,0:T(8,128)(2,1)S(1)}, u32[]{:S(2)}, u32[]{:S(2)}) collective-permute-start(bf16[580,512]{1,0:T(8,128)(2,1)S(1)} %get-tuple-element.60), channel_id=1, source_target_pairs={{192,0},{0,64},{64,128},{128,192},{193,1},{1,65},{65,129},{129,193... | collective-permute-start | bytes 1781768 | tf_op jit(solution)/shard_map/ppermute | solution.py:30
  129.4 16.7 %collective-permute-start.23 = (bf16[608,512]{1,0:T(8,128)(2,1)S(1)}, bf16[608,512]{1,0:T(8,128)(2,1)S(1)}, u32[]{:S(2)}, u32[]{:S(2)}) collective-permute-start(bf16[608,512]{1,0:T(8,128)(2,1)S(1)} %get-tuple-element.59), channel_id=1, source_target_pairs={{64,0},{128,64},{192,128},{0,192},{65,1},{129,65},{193,129},{1,193... | collective-permute-start | bytes 1867784 | tf_op jit(solution)/shard_map/ppermute | solution.py:30
  135.6 7.2 %collective-permute-start.21 = (f32[32,512]{1,0:T(8,128)S(1)}, f32[32,512]{1,0:T(8,128)S(1)}, u32[]{:S(2)}, u32[]{:S(2)}) collective-permute-start(f32[32,512]{1,0:T(8,128)S(1)} %get-tuple-element.67), channel_id=1, source_target_pairs={{32,0},{33,1},{34,2},{35,3},{36,4},{37,5},{38,6},{39,7},{40,8},{41... | collective-permute-start | bytes 196616 | tf_op jit(solution)/shard_map/ppermute | solution.py:26
  135.9 6.9 %collective-permute-start.22 = (f32[32,512]{1,0:T(8,128)S(1)}, f32[32,512]{1,0:T(8,128)S(1)}, u32[]{:S(2)}, u32[]{:S(2)}) collective-permute-start(f32[32,512]{1,0:T(8,128)S(1)} %get-tuple-element.68), channel_id=1, source_target_pairs={{16,0},{17,1},{18,2},{19,3},{20,4},{21,5},{22,6},{23,7},{24,8},{25... | collective-permute-start | bytes 196616 | tf_op jit(solution)/shard_map/ppermute | solution.py:26
  139.2 6.2 %collective-permute-start.20 = (f32[32,512]{1,0:T(8,128)S(1)}, f32[32,512]{1,0:T(8,128)S(1)}, u32[]{:S(2)}, u32[]{:S(2)}) collective-permute-start(f32[32,512]{1,0:T(8,128)S(1)} %get-tuple-element.69), channel_id=1, source_target_pairs={{48,0},{49,1},{50,2},{51,3},{52,4},{53,5},{54,6},{55,7},{56,8},{57... | collective-permute-start | bytes 196616 | tf_op jit(solution)/shard_map/ppermute | solution.py:26
